TPU v7x, 32 devices: a whole 2x2x4 slice. The times are simulated.
32 devices in a mesh: tm: 4 (over y, x), rows: 8 (over z, core).
Axes of the slice: x: 2, y: 2, z: 4, core: 2. Of those that a mesh axis runs over, the one named last changes fastest.
Arguments:
- features: bfloat16 [16, 16, 64, 384], P('tm', 'rows'), may hold values from -6 to 6
- first_weight: bfloat16 [3, 3, 3, 384, 192], replicated, may hold values from -0.0625 to 0.0625
- first_bias: float32 [192], replicated, may hold values from -1.5 to 1.5
- first_gain: float32 [384], replicated, may hold values from 0.25 to 1.75
- second_weight: bfloat16 [3, 3, 3, 192, 192], replicated, may hold values from -0.078125 to 0.078125
- second_bias: float32 [192], replicated, may hold values from -1.5 to 1.5
- second_gain: float32 [192], replicated, may hold values from 0.25 to 1.75
- skip_weight: bfloat16 [384, 192], replicated, may hold values from -0.3125 to 0.3125
- skip_bias: float32 [192], replicated, may hold values from -1.5 to 1.5
Outputs:
- block_out: bfloat16 [16, 16, 64, 192], P('tm', 'rows')
All inputs are finite; a program needn't handle non-finite values.
Results may differ from a plain program's by a relative error of at most 0.01.
Values may be sent and summed in bfloat16 or wider, within the bound.
A program may use at most 64 MiB of HBM per device.

v0:
```python
import jax
import jax.numpy as jnp
from jax import lax
from jax.sharding import PartitionSpec as P


def extended(cells, sides, width):
    for axis, dim in sides:
        count = lax.axis_size(axis)
        ends = count - 1
        head = lax.slice_in_dim(cells, 0, width, axis=dim)
        tail = lax.slice_in_dim(cells, cells.shape[dim] - width, cells.shape[dim], axis=dim)
        cells = jnp.concatenate(
            [
                lax.ppermute(tail, axis, [(i, (i + 1) % count) for i in range(ends)]),
                cells,
                lax.ppermute(head, axis, [((i + 1) % count, i) for i in range(ends)]),
            ],
            axis=dim,
        )
    return cells


def from_behind(value, axis, steps):
    count = lax.axis_size(axis)
    initial, last = (max(0, -steps), min(count, count - steps))
    return lax.ppermute(value, axis, [(source, source + steps) for source in range(initial, last)])


def activate(values, gain):
    floats = values.astype(jnp.float32)
    scaled = floats * lax.rsqrt(jnp.mean(floats * floats, axis=-1, keepdims=True) + 1e-06) * gain
    return jax.nn.silu(scaled).astype(jnp.bfloat16)


def convolve(padded, weight, bias):
    frames = padded.shape[0] - 2
    height = padded.shape[1] - 2
    across = padded.shape[2]
    channels = padded.shape[3]
    outputs = weight.shape[4]
    widened = jnp.pad(padded, ((0, 0), (0, 0), (1, 1), (0, 0)))
    summed = jnp.zeros((frames * height * across, outputs), jnp.float32)
    for time_tap in range(3):
        for row_tap in range(3):
            stacked = jnp.concatenate(
                [
                    widened[
                        time_tap : time_tap + frames,
                        row_tap : row_tap + height,
                        col_tap : col_tap + across,
                    ]
                    for col_tap in range(3)
                ],
                axis=-1,
            )
            summed = summed + jnp.dot(
                stacked.reshape(-1, 3 * channels),
                weight[time_tap, row_tap].reshape(3 * channels, outputs),
                preferred_element_type=jnp.float32,
            )
    return summed.reshape(frames, height, across, outputs) + bias


def per_device(
    features,
    first_weight,
    first_bias,
    first_gain,
    second_weight,
    second_bias,
    second_gain,
    skip_weight,
    skip_bias,
):
    frames = features.shape[0]
    first_act = activate(features, first_gain)
    rimmed = extended(first_act, (("rows", 1),), 1)
    earlier = from_behind(rimmed[frames - 2 :], "tm", 1)
    hidden = convolve(jnp.concatenate([earlier, rimmed], 0), first_weight, first_bias).astype(
        jnp.bfloat16
    )
    second_act = activate(hidden, second_gain)
    rimmed = extended(second_act, (("rows", 1),), 1)
    earlier = from_behind(rimmed[frames - 2 :], "tm", 1)
    branch = convolve(jnp.concatenate([earlier, rimmed], 0), second_weight, second_bias)
    skipped = jnp.dot(
        features.reshape(-1, features.shape[-1]), skip_weight, preferred_element_type=jnp.float32
    )
    skipped = skipped.reshape(branch.shape)
    return (branch + skipped + skip_bias).astype(jnp.bfloat16)


def solution(mesh):
    return jax.shard_map(
        per_device,
        mesh=mesh,
        in_specs=(P("tm", "rows", None, None), P(), P(), P(), P(), P(), P(), P(), P()),
        out_specs=P("tm", "rows", None, None),
        check_vma=False,
    )
```

profile of v0, /device:TPU:12, one launch (start us, length us, event | category | flops | bytes accessed | tf_op | source)
XLA Modules:
  0.0 62.8 jit_solution(8017569776578729442)
XLA Ops:
  0.0 1.2 %fusion.6 = f32[4,2,64]{2,1,0:T(2,128)S(1)} fusion(bf16[4,2,64,384]{3,2,1,0:T(8,128)(2,1)} %param.9), kind=kLoop, calls=%fused_computation.35 | loop fusion | flops 589312 | bytes 395264 | tf_op jit(solution)/shard_map/reduce_sum | solution.py:32
  1.2 1.3 %fusion.13 = bf16[4,2,64,384]{3,2,1,0:T(8,128)(2,1)S(1)} fusion(bf16[4,2,64,384]{3,2,1,0:T(8,128)(2,1)} %param.9, f32[384]{0:T(512)} %param.12, f32[4,2,64]{2,1,0:T(2,128)S(1)} %add_rsqrt_fusion), kind=kLoop, calls=%fused_computation.42 | loop fusion | flops 1572864 | bytes 790016 | tf_op jit(solution)/shard_map/convert_element_type | solution.py:33
  2.6 1.9 %collective-permute-start.1 = (bf16[4,1,64,384]{3,2,1,0:T(8,128)(2,1)S(1)}, bf16[4,1,64,384]{3,2,1,0:T(8,128)(2,1)S(1)}, u32[]{:S(2)}, u32[]{:S(2)}) collective-permute-start(bf16[4,1,64,384]{3,2,1,0:T(8,128)(2,1)S(1)} %get-tuple-element.75), channel_id=1, source_target_pairs={{1,0},{2,1},{3,2},{4,3},{5,4},{6,5},{7,6},{9,8},{10,9},{11,10},{12... | collective-permute-start | bytes 589832 | tf_op jit(solution)/shard_map/ppermute | solution.py:17
  4.5 2.4 %collective-permute-start = (bf16[4,1,64,384]{3,2,1,0:T(8,128)(2,1)S(1)}, bf16[4,1,64,384]{3,2,1,0:T(8,128)(2,1)S(1)}, u32[]{:S(2)}, u32[]{:S(2)}) collective-permute-start(bf16[4,1,64,384]{3,2,1,0:T(8,128)(2,1)S(1)} %get-tuple-element.74), channel_id=1, source_target_pairs={{0,1},{1,2},{2,3},{3,4},{4,5},{5,6},{6,7},{8,9},{9,10},{10,11},{11... | collective-permute-start | bytes 589832 | tf_op jit(solution)/shard_map/ppermute | solution.py:15
  6.9 0.8 %collective-permute-done.1 = bf16[4,1,64,384]{3,2,1,0:T(8,128)(2,1)S(1)} collective-permute-done((bf16[4,1,64,384]{3,2,1,0:T(8,128)(2,1)S(1)}, bf16[4,1,64,384]{3,2,1,0:T(8,128)(2,1)S(1)}, u32[]{:S(2)}, u32[]{:S(2)}) %collective-permute-start.1) | collective-permute-done | bytes 196640 | tf_op jit(solution)/shard_map/ppermute | solution.py:17
  7.7 3.8 %collective-permute-done = bf16[4,1,64,384]{3,2,1,0:T(8,128)(2,1)S(1)} collective-permute-done((bf16[4,1,64,384]{3,2,1,0:T(8,128)(2,1)S(1)}, bf16[4,1,64,384]{3,2,1,0:T(8,128)(2,1)S(1)}, u32[]{:S(2)}, u32[]{:S(2)}) %collective-permute-start) | collective-permute-done | bytes 196640 | tf_op jit(solution)/shard_map/ppermute | solution.py:15
  11.5 3.4 %collective-permute-start.2 = (bf16[2,4,64,384]{3,2,1,0:T(8,128)(2,1)S(1)}, bf16[2,4,64,384]{3,2,1,0:T(8,128)(2,1)S(1)}, u32[]{:S(2)}, u32[]{:S(2)}) collective-permute-start(bf16[2,4,64,384]{3,2,1,0:T(8,128)(2,1)S(1)} %pad_maximum_fusion.18), channel_id=1, source_target_pairs={{0,8},{8,16},{16,24},{1,9},{9,17},{17,25},{2,10},{10,18},{18,26},{... | collective-permute-start | bytes 1179656 | tf_op jit(solution)/shard_map/ppermute | solution.py:27
  15.0 2.5 %fusion.19 = (bf16[1,1,3,384,192]{3,4,2,1,0:T(8,128)(2,1)S(1)}, bf16[1,1,3,384,192]{3,4,2,1,0:T(8,128)(2,1)S(1)}, bf16[1,1,3,384,192]{3,4,2,1,0:T(8,128)(2,1)S(1...) fusion(bf16[3,3,3,384,192]{3,4,2,1,0:T(8,128)(2,1)} %param.10), kind=kLoop, calls=%fused_computation.104 | loop fusion | bytes 7962624 | tf_op jit(solution)/shard_map/slice | solution.py:59
  17.5 0.4 copy.11
  17.9 0.4 copy.12
  18.4 0.4 copy.13
  18.9 0.4 copy.14
  19.3 0.4 copy.15
  19.8 0.4 copy.16
  20.2 0.4 copy.17
  20.7 0.4 copy.18
  21.6 3.0 %collective-permute-done.2 = bf16[2,4,64,384]{3,2,1,0:T(8,128)(2,1)S(1)} collective-permute-done((bf16[2,4,64,384]{3,2,1,0:T(8,128)(2,1)S(1)}, bf16[2,4,64,384]{3,2,1,0:T(8,128)(2,1)S(1)}, u32[]{:S(2)}, u32[]{:S(2)}) %collective-permute-start.2) | collective-permute-done | bytes 393248 | tf_op jit(solution)/shard_map/ppermute | solution.py:27
  24.8 0.8 %pad_slice_fusion.19 = (bf16[4,2,64,384]{3,2,1,0:T(8,128)(2,1)S(1)}, bf16[4,2,64,384]{3,2,1,0:T(8,128)(2,1)S(1)}, bf16[4,2,64,384]{3,2,1,0:T(8,128)(2,1)S(1)}, b...) fusion(bf16[6,4,64,384]{3,2,1,0:T(8,128)(2,1)S(1)} %maximum_max, ...), kind=kLoop, calls=%fused_computation.87 | loop fusion | bytes 5505024 | tf_op jit(solution)/shard_map/slice | solution.py:48
  25.8 0.8 %pad_slice_fusion.18 = (bf16[4,2,64,384]{3,2,1,0:T(8,128)(2,1)S(1)}, bf16[4,2,64,384]{3,2,1,0:T(8,128)(2,1)S(1)}, bf16[4,2,64,384]{3,2,1,0:T(8,128)(2,1)S(1)}, b...) fusion(bf16[6,4,64,384]{3,2,1,0:T(8,128)(2,1)S(1)} %maximum_max, ...), kind=kLoop, calls=%fused_computation.86 | loop fusion | bytes 6684672 | tf_op jit(solution)/shard_map/slice | solution.py:48
  27.0 0.5 fusion.25
  27.5 0.5 convolution_add_fusion.8
  28.4 0.5 convolution_add_fusion.7
  29.0 0.5 convolution_add_fusion.6
  29.9 0.5 convolution_add_fusion.5
  30.4 0.5 convolution_add_fusion.4
  31.0 0.4 fusion.3
  31.4 0.6 convolution_add_fusion.3
  32.0 0.6 convolution_add_fusion.2
  32.7 1.3 %multiply_reduce_fusion = (f32[512]{0:T(512)S(1)}, f32[512,192]{0,1:T(8,128)}) fusion(f32[192]{0:T(256)S(1)} %copy-done.3, f32[512,192]{0,1:T(8,128)S(1)} %convolution_add_fusion.2, bf16[512,1152]{1,0:T(8,128)(2,1)S(1)} %bitcast.116, bf16[1152,192]{0,1:T(8,128)(2,1)S(1)} %bitcast.145), kind=kOutput, calls=%fused_computation.61 | convolution fusion | flops 227081728 | bytes 2411264 | tf_op jit(solution)/shard_map/dot_general | solution.py:57
  34.0 1.3 %copy.20 = f32[512,192]{1,0:T(8,128)S(1)} copy(f32[512,192]{0,1:T(8,128)} %get-tuple-element.82) | data formatting | bytes 786432 | tf_op jit(solution)/shard_map/add | solution.py:57
  35.7 1.9 %collective-permute-start.4 = (bf16[4,1,64,192]{3,2,1,0:T(8,128)(2,1)S(1)}, bf16[4,1,64,192]{3,2,1,0:T(8,128)(2,1)S(1)}, u32[]{:S(2)}, u32[]{:S(2)}) collective-permute-start(bf16[4,1,64,192]{3,2,1,0:T(8,128)(2,1)S(1)} %get-tuple-element.80), channel_id=1, source_target_pairs={{1,0},{2,1},{3,2},{4,3},{5,4},{6,5},{7,6},{9,8},{10,9},{11,10},{12... | collective-permute-start | bytes 294920 | tf_op jit(solution)/shard_map/ppermute | solution.py:17
  37.6 2.4 %collective-permute-start.3 = (bf16[4,1,64,192]{3,2,1,0:T(8,128)(2,1)S(1)}, bf16[4,1,64,192]{3,2,1,0:T(8,128)(2,1)S(1)}, u32[]{:S(2)}, u32[]{:S(2)}) collective-permute-start(bf16[4,1,64,192]{3,2,1,0:T(8,128)(2,1)S(1)} %get-tuple-element.79), channel_id=1, source_target_pairs={{0,1},{1,2},{2,3},{3,4},{4,5},{5,6},{6,7},{8,9},{9,10},{10,11},{11... | collective-permute-start | bytes 294920 | tf_op jit(solution)/shard_map/ppermute | solution.py:15
  40.1 3.8 %collective-permute-done.3 = bf16[4,1,64,192]{3,2,1,0:T(8,128)(2,1)S(1)} collective-permute-done((bf16[4,1,64,192]{3,2,1,0:T(8,128)(2,1)S(1)}, bf16[4,1,64,192]{3,2,1,0:T(8,128)(2,1)S(1)}, u32[]{:S(2)}, u32[]{:S(2)}) %collective-permute-start.3) | collective-permute-done | bytes 98336 | tf_op jit(solution)/shard_map/ppermute | solution.py:15
  44.0 2.7 %collective-permute-start.5 = (bf16[2,4,64,192]{3,2,1,0:T(8,128)(2,1)S(1)}, bf16[2,4,64,192]{3,2,1,0:T(8,128)(2,1)S(1)}, u32[]{:S(2)}, u32[]{:S(2)}) collective-permute-start(bf16[2,4,64,192]{3,2,1,0:T(8,128)(2,1)S(1)} %pad_maximum_fusion.20), channel_id=1, source_target_pairs={{0,8},{8,16},{16,24},{1,9},{9,17},{17,25},{2,10},{10,18},{18,26},{... | collective-permute-start | bytes 589832 | tf_op jit(solution)/shard_map/ppermute | solution.py:27
  46.8 7.4 %collective-permute-done.5 = bf16[2,4,64,192]{3,2,1,0:T(8,128)(2,1)S(1)} collective-permute-done((bf16[2,4,64,192]{3,2,1,0:T(8,128)(2,1)S(1)}, bf16[2,4,64,192]{3,2,1,0:T(8,128)(2,1)S(1)}, u32[]{:S(2)}, u32[]{:S(2)}) %collective-permute-start.5) | collective-permute-done | bytes 196640 | tf_op jit(solution)/shard_map/ppermute | solution.py:27
  54.4 0.5 pad_slice_fusion.1
  55.0 0.5 pad_slice_fusion
  55.7 0.4 fusion.26
  56.3 0.4 convolution_add_fusion.16
  57.0 0.4 convolution_add_fusion.15
  57.6 0.4 convolution_add_fusion.14
  58.2 0.4 convolution_add_fusion.13
  58.8 0.4 convolution_add_fusion.12
  59.2 0.8 %fusion.15 = (bf16[4,2,64,576]{3,2,1,0:T(8,128)(2,1)S(1)}, bf16[4,2,64,576]{3,2,1,0:T(8,128)(2,1)S(1)}, bf16[4,2,64,576]{3,2,1,0:T(8,128)(2,1)S(1)}) fusion(bf16[4,1,64,192]{3,2,1,0:T(8,128)(2,1)S(1)} %collective-permute-done.4, bf16[4,2,64,192]{3,2,1,0:T(8,128)(2,1)S(1)} %multiply_convert_fusion, bf16[4,2,64,192]{3,2,1,0:T(8,128)(2,1)S(1)} %get-tuple-element.57, ...), kind=kLoop, calls=%fused_computation.46 | loop fusion | flops 6488064 | bytes 3342336 | tf_op jit(solution)/shard_map/concatenate | solution.py:46
  60.0 0.4 convolution_add_fusion.11
  60.4 0.4 convolution_add_fusion.10
  60.8 0.4 convolution_add_fusion.9
  61.8 1.0 %fusion.1 = bf16[4,2,64,192]{3,2,1,0:T(8,128)(2,1)} fusion(bf16[4,2,64,384]{3,2,1,0:T(8,128)(2,1)S(1)} %copy-done.1, f32[4,2,64,192]{3,2,1,0:T(8,128)S(1)} %bitcast.144, f32[192]{0:T(256)S(1)} %copy-done.5, f32[192]{0:T(256)S(1)} %copy-done.6, bf16[384,192]{0,1:T(8,128)(2,1)S(1)} %copy-done), kind=kOutput, calls=%fused_computation.2 | convolution fusion | flops 75890688 | bytes 1132032 | tf_op jit(solution)/shard_map/dot_general | solution.py:87
  (48 shorter events, 5.3 us)
Async XLA Ops:
  0.0 61.5 %copy-start = (bf16[384,192]{0,1:T(8,128)(2,1)S(1)}, bf16[384,192]{0,1:T(8,128)(2,1)}, u32[]{:S(2)}) copy-start(bf16[384,192]{0,1:T(8,128)(2,1)} %param.16) | copy-start | bytes 442372
  2.6 5.1 %collective-permute-start.1 = (bf16[4,1,64,384]{3,2,1,0:T(8,128)(2,1)S(1)}, bf16[4,1,64,384]{3,2,1,0:T(8,128)(2,1)S(1)}, u32[]{:S(2)}, u32[]{:S(2)}) collective-permute-start(bf16[4,1,64,384]{3,2,1,0:T(8,128)(2,1)S(1)} %get-tuple-element.75), channel_id=1, source_target_pairs={{1,0},{2,1},{3,2},{4,3},{5,4},{6,5},{7,6},{9,8},{10,9},{11,10},{12... | collective-permute-start | bytes 589832 | tf_op jit(solution)/shard_map/ppermute | solution.py:17
  4.5 7.0 %collective-permute-start = (bf16[4,1,64,384]{3,2,1,0:T(8,128)(2,1)S(1)}, bf16[4,1,64,384]{3,2,1,0:T(8,128)(2,1)S(1)}, u32[]{:S(2)}, u32[]{:S(2)}) collective-permute-start(bf16[4,1,64,384]{3,2,1,0:T(8,128)(2,1)S(1)} %get-tuple-element.74), channel_id=1, source_target_pairs={{0,1},{1,2},{2,3},{3,4},{4,5},{5,6},{6,7},{8,9},{9,10},{10,11},{11... | collective-permute-start | bytes 589832 | tf_op jit(solution)/shard_map/ppermute | solution.py:15
  11.5 13.0 %collective-permute-start.2 = (bf16[2,4,64,384]{3,2,1,0:T(8,128)(2,1)S(1)}, bf16[2,4,64,384]{3,2,1,0:T(8,128)(2,1)S(1)}, u32[]{:S(2)}, u32[]{:S(2)}) collective-permute-start(bf16[2,4,64,384]{3,2,1,0:T(8,128)(2,1)S(1)} %pad_maximum_fusion.18), channel_id=1, source_target_pairs={{0,8},{8,16},{16,24},{1,9},{9,17},{17,25},{2,10},{10,18},{18,26},{... | collective-permute-start | bytes 1179656 | tf_op jit(solution)/shard_map/ppermute | solution.py:27
  32.0 0.7 %copy-start.3 = (f32[192]{0:T(256)S(1)}, f32[192]{0:T(256)}, u32[]{:S(2)}) copy-start(f32[192]{0:T(256)} %param.11) | copy-start | bytes 2308
  32.7 2.8 %copy-start.4 = (f32[192]{0:T(256)S(1)}, f32[192]{0:T(256)}, u32[]{:S(2)}) copy-start(f32[192]{0:T(256)} %param.15) | copy-start | bytes 2308
  34.0 12.7 %copy-start.2 = (bf16[3,3,3,192,192]{4,3,2,1,0:T(8,128)(2,1)S(1)}, bf16[3,3,3,192,192]{4,3,2,1,0:T(8,128)(2,1)}, u32[]{:S(2)}) copy-start(bf16[3,3,3,192,192]{4,3,2,1,0:T(8,128)(2,1)} %param.13) | copy-start | bytes 5971972
  35.7 4.4 %collective-permute-start.4 = (bf16[4,1,64,192]{3,2,1,0:T(8,128)(2,1)S(1)}, bf16[4,1,64,192]{3,2,1,0:T(8,128)(2,1)S(1)}, u32[]{:S(2)}, u32[]{:S(2)}) collective-permute-start(bf16[4,1,64,192]{3,2,1,0:T(8,128)(2,1)S(1)} %get-tuple-element.80), channel_id=1, source_target_pairs={{1,0},{2,1},{3,2},{4,3},{5,4},{6,5},{7,6},{9,8},{10,9},{11,10},{12... | collective-permute-start | bytes 294920 | tf_op jit(solution)/shard_map/ppermute | solution.py:17
  37.6 6.3 %collective-permute-start.3 = (bf16[4,1,64,192]{3,2,1,0:T(8,128)(2,1)S(1)}, bf16[4,1,64,192]{3,2,1,0:T(8,128)(2,1)S(1)}, u32[]{:S(2)}, u32[]{:S(2)}) collective-permute-start(bf16[4,1,64,192]{3,2,1,0:T(8,128)(2,1)S(1)} %get-tuple-element.79), channel_id=1, source_target_pairs={{0,1},{1,2},{2,3},{3,4},{4,5},{5,6},{6,7},{8,9},{9,10},{10,11},{11... | collective-permute-start | bytes 294920 | tf_op jit(solution)/shard_map/ppermute | solution.py:15
  44.0 10.3 %collective-permute-start.5 = (bf16[2,4,64,192]{3,2,1,0:T(8,128)(2,1)S(1)}, bf16[2,4,64,192]{3,2,1,0:T(8,128)(2,1)S(1)}, u32[]{:S(2)}, u32[]{:S(2)}) collective-permute-start(bf16[2,4,64,192]{3,2,1,0:T(8,128)(2,1)S(1)} %pad_maximum_fusion.20), channel_id=1, source_target_pairs={{0,8},{8,16},{16,24},{1,9},{9,17},{17,25},{2,10},{10,18},{18,26},{... | collective-permute-start | bytes 589832 | tf_op jit(solution)/shard_map/ppermute | solution.py:27
  60.8 1.0 %copy-start.1 = (bf16[4,2,64,384]{3,2,1,0:T(8,128)(2,1)S(1)}, bf16[4,2,64,384]{3,2,1,0:T(8,128)(2,1)}, u32[]{:S(2)}) copy-start(bf16[4,2,64,384]{3,2,1,0:T(8,128)(2,1)} %param.9) | copy-start | bytes 1179652
  60.8 1.0 %copy-start.5 = (f32[192]{0:T(256)S(1)}, f32[192]{0:T(256)}, u32[]{:S(2)}) copy-start(f32[192]{0:T(256)} %param.17) | copy-start | bytes 2308
  60.8 1.0 %copy-start.6 = (f32[192]{0:T(256)S(1)}, f32[192]{0:T(256)}, u32[]{:S(2)}) copy-start(f32[192]{0:T(256)} %param.14) | copy-start | bytes 2308
where the time goes:
time: 63.2 us; the launch traced here: 62.8 us
  waiting for transfers between devices  18.8 us (30%)
  starting transfers between devices  14.7 us (23%)
  local copies, waits for them, and re-layouts  11.8 us (19%)
  matrix products  10.3 us (16%)
  other arithmetic  6.7 us (11%)
    ppermute x2, waiting for transfers between devices, from_behind(): lax.ppermute(value, axis, [(source, source + steps) for source in range(i...  10.3 us
    dot_general x18, matrix products, convolve(): jnp.dot(stacked.reshape(-1, 3 * channels), weight[time_tap, row_tap].resh...  9.23 us
    ppermute x2, waiting for transfers between devices, extended(): lax.ppermute(tail, axis, [(i, (i + 1) % count) for i in range(ends)])  7.61 us
    slice x11, local copies, waits for them, and re-layouts, convolve(): weight[time_tap, row_tap].reshape(3 * channels, outputs)  6.14 us
    ppermute x2, starting transfers between devices, from_behind(): lax.ppermute(value, axis, [(source, source + steps) for source in range(i...  6.08 us
    ppermute x2, starting transfers between devices, extended(): lax.ppermute(tail, axis, [(i, (i + 1) % count) for i in range(ends)])  4.81 us
    ppermute x2, starting transfers between devices, extended(): lax.ppermute(head, axis, [((i + 1) % count, i) for i in range(ends)])  3.84 us
    concatenate x11, other arithmetic, convolve(): jnp.concatenate([widened[time_tap:time_tap + frames, row_tap:row_tap + he...  3.53 us
  transfers between devices with their start and end apart: 6, of which 6 were waited for; matrix products, arithmetic and copies ran while one was open for 11% of the time, Pallas kernels for 0%

commit v1 on v0

v1 whole, which is shorter than its diff:
```python
import functools

import jax
import jax.numpy as jnp
from jax import lax
from jax.experimental import pallas as pl
from jax.experimental.pallas import tpu as pltpu
from jax.sharding import PartitionSpec as P

MESH = pl.DeviceIdType.MESH
EDGE = 8


def activate(values, gain):
    floats = values.astype(jnp.float32)
    scaled = floats * lax.rsqrt(jnp.mean(floats * floats, axis=-1, keepdims=True) + 1e-06) * gain
    half = 0.5 * scaled
    return (half + half * jnp.tanh(half)).astype(jnp.bfloat16)


def times_rows(cells, weight):
    return lax.dot_general(
        cells, weight, (((1,), (1,)), ((), ())), preferred_element_type=jnp.float32
    )


def times(cells, weight):
    return jnp.dot(cells, weight, preferred_element_type=jnp.float32)


class Totals:
    def __init__(self, ref, across):
        self.ref, self.across, self.begun = ref, across, set()

    def clear_edges(self):
        shape = self.ref.shape
        zeros = jnp.zeros(shape[1:3] + (EDGE, shape[4]), jnp.float32)
        self.ref[0, :, :, 0:EDGE] = zeros
        self.ref[2, :, :, EDGE + self.across :] = zeros

    def add(self, tap, row, frame, value):
        for offset in range(value.shape[0]):
            key = (tap, row, frame + offset)
            place = (tap, row, frame + offset, pl.ds(EDGE, self.across))
            if key in self.begun:
                self.ref[place] += value[offset]
            else:
                self.begun.add(key)
                self.ref[place] = value[offset]

    def combined(self, row, frame):
        ref, across = self.ref, self.across
        return (
            ref[1, row, frame, pl.ds(EDGE, across)]
            + ref[0, row, frame, pl.ds(EDGE - 1, across)]
            + ref[2, row, frame, pl.ds(EDGE + 1, across)]
        )


def kernel(
    counts, x_hbm, w1_hbm, b1, g1, w2_hbm, b2, g2, ws_hbm, bs, out,
    x, w1, w2, ws, a1, a2, h1, h2, s1, s2, skip, p1, q1, p2, q2,
    load, row_send, row_recv, time_send, time_recv,
):
    ranks, bands = counts
    rank, band = lax.axis_index("tm"), lax.axis_index("rows")
    frames, _, across, inputs = x.shape
    outputs = out.shape[3]
    late = frames - 2
    has_up, has_down = band > 0, band < bands - 1
    has_before, has_after = rank > 0, rank < ranks - 1
    up = {"tm": rank, "rows": band - 1}
    down = {"tm": rank, "rows": band + 1}
    before = {"tm": rank - 1, "rows": band}
    after = {"tm": rank + 1, "rows": band}

    loads = [pltpu.make_async_copy(x_hbm, x, load.at[0])]
    for i in range(3):
        loads.append(pltpu.make_async_copy(w1_hbm.at[i], w1.at[i], load.at[1 + i]))
    loads.append(pltpu.make_async_copy(ws_hbm, ws, load.at[4]))
    loads.append(pltpu.make_async_copy(w2_hbm, w2, load.at[5]))
    for copy in loads:
        copy.start()

    barrier = pltpu.get_barrier_semaphore()
    for there, device in ((has_up, up), (has_down, down), (has_before, before), (has_after, after)):

        @pl.when(there)
        def _(device=device):
            pl.semaphore_signal(barrier, inc=1, device_id=device, device_id_type=MESH)

    @pl.when(jnp.logical_not(has_up))
    def _():
        h1[0] = jnp.zeros_like(h1[0])
        h2[0] = jnp.zeros_like(h2[0])

    @pl.when(jnp.logical_not(has_down))
    def _():
        h1[1] = jnp.zeros_like(h1[1])
        h2[1] = jnp.zeros_like(h2[1])

    @pl.when(jnp.logical_not(has_before))
    def _():
        q1[...] = jnp.zeros_like(q1)
        q2[...] = jnp.zeros_like(q2)

    t1, t2 = Totals(s1, across), Totals(s2, across)
    t1.clear_edges()
    t2.clear_edges()

    def row_copies(step, span):
        part = 2 * step + (1 if span[0] == 0 else 0)
        cut = pl.ds(span[0], span[1] - span[0])
        if step == 0:
            first, last = a1.at[cut, :, 0:inputs], a1.at[cut, :, inputs : 2 * inputs]
            halo = h1
        else:
            first, last, halo = a2.at[0, cut], a2.at[1, cut], h2
        upward = pltpu.make_async_remote_copy(
            first, halo.at[1, cut], row_send.at[part, 0], row_recv.at[part, 1],
            device_id=up, device_id_type=MESH,
        )
        downward = pltpu.make_async_remote_copy(
            last, halo.at[0, cut], row_send.at[part, 1], row_recv.at[part, 0],
            device_id=down, device_id_type=MESH,
        )
        return upward, downward

    def send_rows(step, span):
        upward, downward = row_copies(step, span)
        pl.when(has_up)(upward.start)
        pl.when(has_down)(downward.start)

    def receive_rows(step, span):
        upward, downward = row_copies(step, span)
        pl.when(has_down)(upward.wait_recv)
        pl.when(has_up)(downward.wait_recv)

    def time_copy(step):
        source, target = ((p1, q1), (p2, q2))[step]
        return pltpu.make_async_remote_copy(
            source, target, time_send.at[step], time_recv.at[step],
            device_id=after, device_id_type=MESH,
        )

    early_span, late_span = (0, late), (late, frames)

    def first_act(span):
        for f in range(*span):
            for r in range(2):
                a1[f, :, r * inputs : (r + 1) * inputs] = activate(x[f, r], g1[...])

    loads[0].wait()
    first_act(late_span)
    pl.semaphore_wait(
        barrier,
        has_up.astype(jnp.int32) + has_down.astype(jnp.int32)
        + has_before.astype(jnp.int32) + has_after.astype(jnp.int32),
    )
    send_rows(0, late_span)
    first_act(early_span)
    send_rows(0, early_span)

    def split(value, span):
        return value.reshape(span[1] - span[0], across, outputs)

    def local1(i, span):
        cells = a1[span[0] : span[1]].reshape(-1, 2 * inputs)
        for k in range(3):
            for r in range(2):
                weight = jnp.concatenate([w1[i, 1 - r, k], w1[i, 2 - r, k]], axis=-1)
                t1.add(k, r, span[0] + 2 - i, split(times_rows(cells, weight), span))

    def halo1(i, span):
        for r in range(2):
            cells = h1[r, span[0] : span[1]].reshape(-1, inputs)
            for k in range(3):
                t1.add(k, r, span[0] + 2 - i, split(times_rows(cells, w1[i, 2 * r, k]), span))

    def local2(i, span):
        top = a2[0, span[0] : span[1]].reshape(-1, outputs)
        low = a2[1, span[0] : span[1]].reshape(-1, outputs)
        for k in range(3):
            for r in range(2):
                value = times(top, w2[i, 1 - r, k]) + times(low, w2[i, 2 - r, k])
                t2.add(k, r, span[0] + 2 - i, split(value, span))

    def halo2(i, span):
        for r in range(2):
            cells = h2[r, span[0] : span[1]].reshape(-1, outputs)
            for k in range(3):
                t2.add(k, r, span[0] + 2 - i, split(times(cells, w2[i, 2 * r, k]), span))

    def send_time(step):
        total, source = ((t1, p1), (t2, p2))[step]
        for f in range(2):
            for r in range(2):
                source[f, r] = total.combined(r, frames + f).astype(jnp.bfloat16)
        pl.when(has_after)(time_copy(step).start)

    def second_act(span):
        for f in range(*span):
            for r in range(2):
                value = t1.combined(r, f) + b1[...]
                if f < 2:
                    value = value + q1[f, r].astype(jnp.float32)
                a2[r, f] = activate(value.astype(jnp.bfloat16), g2[...])

    def finish(span):
        for f in range(*span):
            for r in range(2):
                value = t2.combined(r, f) + skip[f, r] + (b2[...] + bs[...])
                if f < 2:
                    value = value + q2[f, r].astype(jnp.float32)
                out[f, r] = value.astype(out.dtype)

    whole = (0, frames)
    for i in range(2):
        loads[1 + i].wait()
        local1(i, whole)
    receive_rows(0, late_span)
    halo1(0, late_span)
    halo1(1, late_span)
    send_time(0)
    loads[3].wait()
    local1(2, whole)
    receive_rows(0, early_span)
    halo1(0, early_span)
    halo1(1, early_span)
    halo1(2, whole)
    second_act(late_span)
    send_rows(1, late_span)

    loads[5].wait()
    for i in range(3):
        local2(i, late_span)
    loads[4].wait()
    skip[...] = times_rows(x[...].reshape(-1, inputs), ws[...]).reshape(skip.shape)

    pl.when(has_before)(time_copy(0).wait_recv)
    second_act(early_span)
    send_rows(1, early_span)
    receive_rows(1, late_span)
    halo2(0, late_span)
    halo2(1, late_span)
    send_time(1)
    halo2(2, late_span)
    for i in range(3):
        local2(i, early_span)
    receive_rows(1, early_span)
    for i in range(3):
        halo2(i, early_span)
    finish(late_span)
    pl.when(has_before)(time_copy(1).wait_recv)
    finish(early_span)

    for step in range(2):
        pl.when(has_after)(time_copy(step).wait_send)
        for span in (late_span, early_span):
            upward, downward = row_copies(step, span)
            pl.when(has_up)(upward.wait_send)
            pl.when(has_down)(downward.wait_send)


def per_device(counts, features, w1, b1, g1, w2, b2, g2, ws, bs):
    frames, height, across, inputs = features.shape
    outputs = w1.shape[4]
    bf16, f32 = jnp.bfloat16, jnp.float32
    any_space = pl.BlockSpec(memory_space=pl.ANY)
    vmem = pl.BlockSpec(memory_space=pltpu.VMEM)
    totals = pltpu.VMEM((3, height, frames + 2, across + 2 * EDGE, outputs), f32)
    passed = pltpu.VMEM((2, height, across, outputs), bf16)
    return pl.pallas_call(
        functools.partial(kernel, counts),
        out_shape=jax.ShapeDtypeStruct((frames, height, across, outputs), bf16),
        in_specs=[any_space, any_space, vmem, vmem, any_space, vmem, vmem, any_space, vmem],
        out_specs=vmem,
        scratch_shapes=[
            pltpu.VMEM(features.shape, bf16),
            pltpu.VMEM((3, 3, 3, outputs, inputs), bf16),
            pltpu.VMEM((3, 3, 3, outputs, outputs), bf16),
            pltpu.VMEM((outputs, inputs), bf16),
            pltpu.VMEM((frames, across, 2 * inputs), bf16),
            pltpu.VMEM((2, frames, across, outputs), bf16),
            pltpu.VMEM((2, frames, across, inputs), bf16),
            pltpu.VMEM((2, frames, across, outputs), bf16),
            totals,
            totals,
            pltpu.VMEM((frames, height, across, outputs), f32),
            passed, passed, passed, passed,
            pltpu.SemaphoreType.DMA((6,)),
            pltpu.SemaphoreType.DMA((4, 2)),
            pltpu.SemaphoreType.DMA((4, 2)),
            pltpu.SemaphoreType.DMA((2,)),
            pltpu.SemaphoreType.DMA((2,)),
        ],
        compiler_params=pltpu.CompilerParams(
            collective_id=0, has_side_effects=True, vmem_limit_bytes=40 * 1024 * 1024
        ),
        name="block",
    )(
        features,
        jnp.swapaxes(w1, 3, 4),
        b1.reshape(1, -1),
        g1.reshape(1, -1),
        w2,
        b2.reshape(1, -1),
        g2.reshape(1, -1),
        jnp.swapaxes(ws, 0, 1),
        bs.reshape(1, -1),
    )


def solution(mesh):
    counts = (mesh.shape["tm"], mesh.shape["rows"])
    return jax.shard_map(
        functools.partial(per_device, counts),
        mesh=mesh,
        in_specs=(P("tm", "rows", None, None), P(), P(), P(), P(), P(), P(), P(), P()),
        out_specs=P("tm", "rows", None, None),
        check_vma=False,
    )
```

time: 63.2 us -> 28.1 us (0.44)
  waiting for transfers between devices: 18.8 us -> 0 us
  Pallas kernels: 0 us -> 17.9 us
  starting transfers between devices: 14.7 us -> 0 us
  matrix products: 10.3 us -> 0 us
  other arithmetic: 6.7 us -> 0 us
  local copies, waits for them, and re-layouts: 11.8 us -> 9.88 us
    ppermute x6 -> x0, waiting for transfers between devices: 18.8 us -> none  [the longest x2 10.3 us: from_behind(): lax.ppermute(value, axis, [(source, source + steps) for source in range(i...]
    pallas_call x0 -> x1, Pallas kernels: none -> 17.9 us  [per_device(): pl.pallas_call(functools.partial(kernel, counts), out_shape=jax.ShapeDtyp...]
    ppermute x6 -> x0, starting transfers between devices: 14.7 us -> none  [the longest x2 6.08 us: from_behind(): lax.ppermute(value, axis, [(source, source + steps) for source in range(i...]
    dot_general x19 -> x0, matrix products: 10.3 us -> none  [the longest x18 9.23 us: convolve(): jnp.dot(stacked.reshape(-1, 3 * channels), weight[time_tap, row_tap].resh...]
    slice x19 -> x0, local copies, waits for them, and re-layouts: 9.13 us -> none  [the longest x11 6.14 us: convolve(): weight[time_tap, row_tap].reshape(3 * channels, outputs)]
    unnamed x23 -> x17, local copies, waits for them, and re-layouts: 1.04 us -> 9.2 us
    concatenate x15 -> x0, other arithmetic: 3.98 us -> none  [the longest x11 3.53 us: convolve(): jnp.concatenate([widened[time_tap:time_tap + frames, row_tap:row_tap + he...]
    add x2 -> x0, local copies, waits for them, and re-layouts: 1.54 us -> none  [convolve(): summed + jnp.dot(stacked.reshape(-1, 3 * channels), weight[time_tap, row_...]
  transfers between devices with their start and end apart: 6 -> 0, of which waited for: 6 -> 0; matrix products, arithmetic and copies ran while one was open for 11% -> 0% of each run, Pallas kernels for 0% -> 0%
where the time goes in v1:
time: 28.1 us; the launch traced here: 27.8 us
  Pallas kernels  17.9 us (64%)
  local copies, waits for them, and re-layouts  9.88 us (35%)
    pallas_call x1, Pallas kernels, per_device(): pl.pallas_call(functools.partial(kernel, counts), out_shape=jax.ShapeDtyp...  17.9 us
    unnamed x17, local copies, waits for them, and re-layouts  9.2 us
    reshape x1, local copies, waits for them, and re-layouts, per_device(): g1.reshape(1, -1)  0.68 us

profile of v1, /device:TPU:12, one launch (start us, length us, event | category | flops | bytes accessed | tf_op | source)
XLA Modules:
  0.0 27.8 jit_solution(12884048816901849649)
XLA Ops:
  0.0 0.7 %reshape.16.g1 = f32[1,384]{1,0:T(1,128)S(1)} reshape(f32[384]{0:T(512)} %param.12) | data formatting | bytes 3072 | tf_op jit(solution)/shard_map/reshape | solution.py:305
  0.7 0.0 copy-start
  0.7 2.1 %copy-done = bf16[3,3,3,384,192]{3,4,2,1,0:T(8,128)(2,1)S(1)} copy-done((bf16[3,3,3,384,192]{3,4,2,1,0:T(8,128)(2,1)S(1)}, bf16[3,3,3,384,192]{3,4,2,1,0:T(8,128)(2,1)}, u32[]{:S(2)}) %copy-start) | copy-done | bytes 3981336
  2.8 0.0 copy-start.1
  2.8 1.7 %copy-done.1 = bf16[3,3,3,192,192]{4,3,2,1,0:T(8,128)(2,1)S(1)} copy-done((bf16[3,3,3,192,192]{4,3,2,1,0:T(8,128)(2,1)S(1)}, bf16[3,3,3,192,192]{4,3,2,1,0:T(8,128)(2,1)}, u32[]{:S(2)}) %copy-start.1) | copy-done | bytes 1990680
  4.6 0.0 copy-start.2
  4.6 1.0 %copy-done.2 = bf16[4,2,64,384]{3,2,1,0:T(8,128)(2,1)S(1)} copy-done((bf16[4,2,64,384]{3,2,1,0:T(8,128)(2,1)S(1)}, bf16[4,2,64,384]{3,2,1,0:T(8,128)(2,1)}, u32[]{:S(2)}) %copy-start.2) | copy-done | bytes 393240
  5.6 0.0 copy-start.3
  5.6 0.9 %copy-done.3 = bf16[384,192]{0,1:T(8,128)(2,1)S(1)} copy-done((bf16[384,192]{0,1:T(8,128)(2,1)S(1)}, bf16[384,192]{0,1:T(8,128)(2,1)}, u32[]{:S(2)}) %copy-start.3) | copy-done | bytes 147480
  6.5 0.0 copy-start.4
  6.5 0.7 %copy-done.4 = f32[192]{0:T(256)S(1)} copy-done((f32[192]{0:T(256)S(1)}, f32[192]{0:T(256)}, u32[]{:S(2)}) %copy-start.4) | copy-done | bytes 792
  7.1 0.0 copy-start.5
  7.2 0.7 %copy-done.5 = f32[192]{0:T(256)S(1)} copy-done((f32[192]{0:T(256)S(1)}, f32[192]{0:T(256)}, u32[]{:S(2)}) %copy-start.5) | copy-done | bytes 792
  7.8 0.0 copy-start.6
  7.8 0.7 %copy-done.6 = f32[192]{0:T(256)S(1)} copy-done((f32[192]{0:T(256)S(1)}, f32[192]{0:T(256)}, u32[]{:S(2)}) %copy-start.6) | copy-done | bytes 792
  8.5 0.0 copy-start.7
  8.5 0.7 %copy-done.7 = f32[192]{0:T(256)S(1)} copy-done((f32[192]{0:T(256)S(1)}, f32[192]{0:T(256)}, u32[]{:S(2)}) %copy-start.7) | copy-done | bytes 792
  9.2 17.9 %block.1 = bf16[4,2,64,192]{3,2,1,0:T(8,128)(2,1)S(1)} custom-call(bf16[4,2,64,384]{3,2,1,0:T(8,128)(2,1)S(1)} %copy-done.2, bf16[3,3,3,192,384]{4,3,2,1,0:T(8,128)(2,1)S(1)} %bitcast.6, f32[1,192]{1,0:T(1,128)S(1)} %bitcast.8, f32[1,384]{1,0:T(1,128)S(1)} %reshape.16.g1, bf16[3,3,3,192,192]{4,3,2,1,0:T(8,128)(2,1)S(1)} %copy-done.1, f32[1,192]{1,0:T(1,128)S(1)} %bitcast.9, ...), custom_call_target="tpu_custom_call" | custom-call | tf_op jit(solution)/shard_map/block/pallas_call | solution.py:273
  27.1 0.7 %copy.11 = bf16[4,2,64,192]{3,2,1,0:T(8,128)(2,1)} copy(bf16[4,2,64,192]{3,2,1,0:T(8,128)(2,1)S(1)} %block.1) | data formatting | bytes 393216
Async XLA Ops:
  0.7 2.1 %copy-start = (bf16[3,3,3,384,192]{3,4,2,1,0:T(8,128)(2,1)S(1)}, bf16[3,3,3,384,192]{3,4,2,1,0:T(8,128)(2,1)}, u32[]{:S(2)}) copy-start(bf16[3,3,3,384,192]{3,4,2,1,0:T(8,128)(2,1)} %param.10) | copy-start | bytes 11943940
  2.8 1.7 %copy-start.1 = (bf16[3,3,3,192,192]{4,3,2,1,0:T(8,128)(2,1)S(1)}, bf16[3,3,3,192,192]{4,3,2,1,0:T(8,128)(2,1)}, u32[]{:S(2)}) copy-start(bf16[3,3,3,192,192]{4,3,2,1,0:T(8,128)(2,1)} %w2_hbm.1) | copy-start | bytes 5971972
  4.6 1.0 %copy-start.2 = (bf16[4,2,64,384]{3,2,1,0:T(8,128)(2,1)S(1)}, bf16[4,2,64,384]{3,2,1,0:T(8,128)(2,1)}, u32[]{:S(2)}) copy-start(bf16[4,2,64,384]{3,2,1,0:T(8,128)(2,1)} %x_hbm.1) | copy-start | bytes 1179652
  5.6 0.9 %copy-start.3 = (bf16[384,192]{0,1:T(8,128)(2,1)S(1)}, bf16[384,192]{0,1:T(8,128)(2,1)}, u32[]{:S(2)}) copy-start(bf16[384,192]{0,1:T(8,128)(2,1)} %param.16) | copy-start | bytes 442372
  6.5 0.7 %copy-start.4 = (f32[192]{0:T(256)S(1)}, f32[192]{0:T(256)}, u32[]{:S(2)}) copy-start(f32[192]{0:T(256)} %param.11) | copy-start | bytes 2308
  7.1 0.7 %copy-start.5 = (f32[192]{0:T(256)S(1)}, f32[192]{0:T(256)}, u32[]{:S(2)}) copy-start(f32[192]{0:T(256)} %param.14) | copy-start | bytes 2308
  7.8 0.7 %copy-start.6 = (f32[192]{0:T(256)S(1)}, f32[192]{0:T(256)}, u32[]{:S(2)}) copy-start(f32[192]{0:T(256)} %param.15) | copy-start | bytes 2308
  8.5 0.7 %copy-start.7 = (f32[192]{0:T(256)S(1)}, f32[192]{0:T(256)}, u32[]{:S(2)}) copy-start(f32[192]{0:T(256)} %param.17) | copy-start | bytes 2308

commit v2 on v1

--- a/solution.py
+++ b/solution.py
@@ -58,8 +58,8 @@
 
 
 def kernel(
-    counts, x_hbm, w1_hbm, b1, g1, w2_hbm, b2, g2, ws_hbm, bs, out,
-    x, w1, w2, ws, a1, a2, h1, h2, s1, s2, skip, p1, q1, p2, q2,
+    counts, x_hbm, w1_hbm, b1_hbm, g1_hbm, w2_hbm, b2_hbm, g2_hbm, ws_hbm, bs_hbm, out,
+    b1, g1, b2, g2, bs, x, w1, w2, ws, a1, a2, h1, h2, s1, s2, skip, p1, q1, p2, q2,
     load, row_send, row_recv, time_send, time_recv,
 ):
     ranks, bands = counts
@@ -79,8 +79,12 @@
         loads.append(pltpu.make_async_copy(w1_hbm.at[i], w1.at[i], load.at[1 + i]))
     loads.append(pltpu.make_async_copy(ws_hbm, ws, load.at[4]))
     loads.append(pltpu.make_async_copy(w2_hbm, w2, load.at[5]))
+    vectors = ((g1_hbm, g1), (b1_hbm, b1), (g2_hbm, g2), (b2_hbm, b2), (bs_hbm, bs))
+    for index, (source, target) in enumerate(vectors):
+        loads.insert(1 + index, pltpu.make_async_copy(source, target, load.at[6 + index]))
     for copy in loads:
         copy.start()
+    small, loads = loads[1:6], loads[:1] + loads[6:]
 
     barrier = pltpu.get_barrier_semaphore()
     for there, device in ((has_up, up), (has_down, down), (has_before, before), (has_after, after)):
@@ -148,9 +152,11 @@
     def first_act(span):
         for f in range(*span):
             for r in range(2):
-                a1[f, :, r * inputs : (r + 1) * inputs] = activate(x[f, r], g1[...])
+                a1[f, :, r * inputs : (r + 1) * inputs] = activate(x[f, r], g1[...].reshape(1, -1))
 
     loads[0].wait()
+    for copy in small:
+        copy.wait()
     first_act(late_span)
     pl.semaphore_wait(
         barrier,
@@ -201,15 +207,15 @@
     def second_act(span):
         for f in range(*span):
             for r in range(2):
-                value = t1.combined(r, f) + b1[...]
+                value = t1.combined(r, f) + b1[...].reshape(1, -1)
                 if f < 2:
                     value = value + q1[f, r].astype(jnp.float32)
-                a2[r, f] = activate(value.astype(jnp.bfloat16), g2[...])
+                a2[r, f] = activate(value.astype(jnp.bfloat16), g2[...].reshape(1, -1))
 
     def finish(span):
         for f in range(*span):
             for r in range(2):
-                value = t2.combined(r, f) + skip[f, r] + (b2[...] + bs[...])
+                value = t2.combined(r, f) + skip[f, r] + (b2[...].reshape(1, -1) + bs[...].reshape(1, -1))
                 if f < 2:
                     value = value + q2[f, r].astype(jnp.float32)
                 out[f, r] = value.astype(out.dtype)
@@ -232,7 +238,7 @@
     send_rows(1, late_span)
 
     loads[5].wait()
-    for i in range(3):
+    for i in range(2):
         local2(i, late_span)
     loads[4].wait()
     skip[...] = times_rows(x[...].reshape(-1, inputs), ws[...]).reshape(skip.shape)
@@ -244,11 +250,12 @@
     halo2(0, late_span)
     halo2(1, late_span)
     send_time(1)
-    halo2(2, late_span)
-    for i in range(3):
+    local2(2, whole)
+    for i in range(2):
         local2(i, early_span)
     receive_rows(1, early_span)
-    for i in range(3):
+    halo2(2, whole)
+    for i in range(2):
         halo2(i, early_span)
     finish(late_span)
     pl.when(has_before)(time_copy(1).wait_recv)
@@ -266,16 +273,21 @@
     frames, height, across, inputs = features.shape
     outputs = w1.shape[4]
     bf16, f32 = jnp.bfloat16, jnp.float32
-    any_space = pl.BlockSpec(memory_space=pl.ANY)
+    hbm = pl.BlockSpec(memory_space=pltpu.HBM)
     vmem = pl.BlockSpec(memory_space=pltpu.VMEM)
     totals = pltpu.VMEM((3, height, frames + 2, across + 2 * EDGE, outputs), f32)
     passed = pltpu.VMEM((2, height, across, outputs), bf16)
     return pl.pallas_call(
         functools.partial(kernel, counts),
         out_shape=jax.ShapeDtypeStruct((frames, height, across, outputs), bf16),
-        in_specs=[any_space, any_space, vmem, vmem, any_space, vmem, vmem, any_space, vmem],
+        in_specs=[hbm] * 9,
         out_specs=vmem,
         scratch_shapes=[
+            pltpu.VMEM(b1.shape, f32),
+            pltpu.VMEM(g1.shape, f32),
+            pltpu.VMEM(b2.shape, f32),
+            pltpu.VMEM(g2.shape, f32),
+            pltpu.VMEM(bs.shape, f32),
             pltpu.VMEM(features.shape, bf16),
             pltpu.VMEM((3, 3, 3, outputs, inputs), bf16),
             pltpu.VMEM((3, 3, 3, outputs, outputs), bf16),
@@ -288,26 +300,26 @@
             totals,
             pltpu.VMEM((frames, height, across, outputs), f32),
             passed, passed, passed, passed,
-            pltpu.SemaphoreType.DMA((6,)),
+            pltpu.SemaphoreType.DMA((11,)),
             pltpu.SemaphoreType.DMA((4, 2)),
             pltpu.SemaphoreType.DMA((4, 2)),
             pltpu.SemaphoreType.DMA((2,)),
             pltpu.SemaphoreType.DMA((2,)),
         ],
         compiler_params=pltpu.CompilerParams(
-            collective_id=0, has_side_effects=True, vmem_limit_bytes=40 * 1024 * 1024
+            collective_id=0, has_side_effects=True, vmem_limit_bytes=64 * 1024 * 1024
         ),
         name="block",
     )(
         features,
         jnp.swapaxes(w1, 3, 4),
-        b1.reshape(1, -1),
-        g1.reshape(1, -1),
+        b1,
+        g1,
         w2,
-        b2.reshape(1, -1),
-        g2.reshape(1, -1),
+        b2,
+        g2,
         jnp.swapaxes(ws, 0, 1),
-        bs.reshape(1, -1),
+        bs,
     )
 
 

time: 28.1 us -> 19.5 us (0.69)
  local copies, waits for them, and re-layouts: 9.88 us -> 1.67 us
    unnamed x17 -> x1, local copies, waits for them, and re-layouts: 9.2 us -> 1.67 us
    reshape x1 -> x0, local copies, waits for them, and re-layouts: 0.68 us -> none  [per_device(): g1.reshape(1, -1)]
where the time goes in v2:
time: 19.5 us; the launch traced here: 19.4 us
  Pallas kernels  17.7 us (91%)
  local copies, waits for them, and re-layouts  1.67 us (9%)
    pallas_call x1, Pallas kernels, per_device(): pl.pallas_call(functools.partial(kernel, counts), out_shape=jax.ShapeDtyp...  17.7 us
    unnamed x1, local copies, waits for them, and re-layouts  1.67 us

profile of v2, /device:TPU:12, one launch (start us, length us, event | category | flops | bytes accessed | tf_op | source)
XLA Modules:
  0.0 19.4 jit_solution(17949348158555766935)
XLA Ops:
  0.0 17.7 %block.1 = bf16[4,2,64,192]{3,2,1,0:T(8,128)(2,1)} custom-call(bf16[4,2,64,384]{3,2,1,0:T(8,128)(2,1)} %x_hbm.1, bf16[3,3,3,192,384]{4,3,2,1,0:T(8,128)(2,1)} %bitcast.2, f32[192]{0:T(256)} %b1_hbm.1, f32[384]{0:T(512)} %g1_hbm.1, bf16[3,3,3,192,192]{4,3,2,1,0:T(8,128)(2,1)} %w2_hbm.1, f32[192]{0:T(256)} %b2_hbm.1, f32[192]{0:T(256)} %g2_hbm.1, ...), custom_call_target="tpu_custom_call" | custom-call | tf_op jit(solution)/shard_map/block/pallas_call | solution.py:280
  17.7 1.7 %copy.11 = bf16[4,2,64,192]{3,2,1,0:T(8,128)(2,1)} copy(bf16[4,2,64,192]{3,2,1,0:T(8,128)(2,1)} %block.1) | data formatting | bytes 393216

commit v3 on v2

--- a/solution.py
+++ b/solution.py
@@ -108,8 +108,7 @@
         q1[...] = jnp.zeros_like(q1)
         q2[...] = jnp.zeros_like(q2)
 
-    t1, t2 = Totals(s1, across), Totals(s2, across)
-    t1.clear_edges()
+    t2 = Totals(s2, across)
     t2.clear_edges()
 
     def row_copies(step, span):
@@ -170,18 +169,40 @@
     def split(value, span):
         return value.reshape(span[1] - span[0], across, outputs)
 
-    def local1(i, span):
-        cells = a1[span[0] : span[1]].reshape(-1, 2 * inputs)
+    lane = lax.broadcasted_iota(jnp.int32, (1, 2 * across), 1)
+    column = lax.rem(lane, across)
+    pair = 2 * across
+
+    def local1(i):
+        cells = a1[...].reshape(-1, 2 * inputs)
+        for r in range(2):
+            weight = jnp.concatenate([w1[i, 1 - r], w1[i, 2 - r]], axis=-1)
+            value = times_rows(weight.reshape(-1, 2 * inputs), cells)
+            s1[r, i] = value.reshape(3, outputs, -1)
+
+    def halo1(i):
+        for r in range(2):
+            cells = h1[r].reshape(-1, inputs)
+            value = times_rows(w1[i, 2 * r].reshape(-1, inputs), cells)
+            s1[r, i] += value.reshape(3, outputs, -1)
+
+    def turned(r, k, half):
+        return pltpu.roll(s1[r, 1, k, :, half * pair : (half + 1) * pair], across, 1)
+
+    def first_sum(r, group):
+        taps = []
         for k in range(3):
-            for r in range(2):
-                weight = jnp.concatenate([w1[i, 1 - r, k], w1[i, 2 - r, k]], axis=-1)
-                t1.add(k, r, span[0] + 2 - i, split(times_rows(cells, weight), span))
-
-    def halo1(i, span):
-        for r in range(2):
-            cells = h1[r, span[0] : span[1]].reshape(-1, inputs)
-            for k in range(3):
-                t1.add(k, r, span[0] + 2 - i, split(times_rows(cells, w1[i, 2 * r, k]), span))
+            if group == 0:
+                total = s1[r, 2, k, :, 0:pair] + jnp.where(lane >= across, turned(r, k, 0), 0.0)
+            elif group == 1:
+                total = s1[r, 2, k, :, pair:] + s1[r, 0, k, :, 0:pair]
+                total += jnp.where(lane < across, turned(r, k, 0), turned(r, k, 1))
+            else:
+                total = s1[r, 0, k, :, pair:] + jnp.where(lane < across, turned(r, k, 1), 0.0)
+            taps.append(total)
+        from_left = jnp.where(column > 0, pltpu.roll(taps[0], 1, 1), 0.0)
+        from_right = jnp.where(column < across - 1, pltpu.roll(taps[2], pair - 1, 1), 0.0)
+        return taps[1] + from_left + from_right
 
     def local2(i, span):
         top = a2[0, span[0] : span[1]].reshape(-1, outputs)
@@ -198,19 +219,24 @@
                 t2.add(k, r, span[0] + 2 - i, split(times(cells, w2[i, 2 * r, k]), span))
 
     def send_time(step):
-        total, source = ((t1, p1), (t2, p2))[step]
-        for f in range(2):
-            for r in range(2):
-                source[f, r] = total.combined(r, frames + f).astype(jnp.bfloat16)
+        for r in range(2):
+            if step == 0:
+                p1[r] = first_sum(r, 2).astype(jnp.bfloat16)
+            else:
+                for f in range(2):
+                    p2[f, r] = t2.combined(r, frames + f).astype(jnp.bfloat16)
         pl.when(has_after)(time_copy(step).start)
 
-    def second_act(span):
-        for f in range(*span):
-            for r in range(2):
-                value = t1.combined(r, f) + b1[...].reshape(1, -1)
-                if f < 2:
-                    value = value + q1[f, r].astype(jnp.float32)
-                a2[r, f] = activate(value.astype(jnp.bfloat16), g2[...].reshape(1, -1))
+    def second_act(group):
+        for r in range(2):
+            value = first_sum(r, group)
+            if group == 0:
+                value = value + q1[r].astype(jnp.float32)
+            spare = jnp.zeros((-outputs % 128, pair), jnp.float32)
+            value = jnp.concatenate([value, spare], axis=0).T[:, :outputs]
+            value = value + b1[...].reshape(1, -1)
+            act = activate(value.astype(jnp.bfloat16), g2[...].reshape(1, -1))
+            a2[r, 2 * group : 2 * group + 2] = act.reshape(2, across, outputs)
 
     def finish(span):
         for f in range(*span):
@@ -223,18 +249,16 @@
     whole = (0, frames)
     for i in range(2):
         loads[1 + i].wait()
-        local1(i, whole)
+        local1(i)
     receive_rows(0, late_span)
-    halo1(0, late_span)
-    halo1(1, late_span)
+    receive_rows(0, early_span)
+    halo1(0)
+    halo1(1)
     send_time(0)
     loads[3].wait()
-    local1(2, whole)
-    receive_rows(0, early_span)
-    halo1(0, early_span)
-    halo1(1, early_span)
-    halo1(2, whole)
-    second_act(late_span)
+    local1(2)
+    halo1(2)
+    second_act(1)
     send_rows(1, late_span)
 
     loads[5].wait()
@@ -244,7 +268,7 @@
     skip[...] = times_rows(x[...].reshape(-1, inputs), ws[...]).reshape(skip.shape)
 
     pl.when(has_before)(time_copy(0).wait_recv)
-    second_act(early_span)
+    second_act(0)
     send_rows(1, early_span)
     receive_rows(1, late_span)
     halo2(0, late_span)
@@ -277,6 +301,7 @@
     vmem = pl.BlockSpec(memory_space=pltpu.VMEM)
     totals = pltpu.VMEM((3, height, frames + 2, across + 2 * EDGE, outputs), f32)
     passed = pltpu.VMEM((2, height, across, outputs), bf16)
+    turned = pltpu.VMEM((height, outputs, 2 * across), bf16)
     return pl.pallas_call(
         functools.partial(kernel, counts),
         out_shape=jax.ShapeDtypeStruct((frames, height, across, outputs), bf16),
@@ -296,10 +321,10 @@
             pltpu.VMEM((2, frames, across, outputs), bf16),
             pltpu.VMEM((2, frames, across, inputs), bf16),
             pltpu.VMEM((2, frames, across, outputs), bf16),
-            totals,
+            pltpu.VMEM((height, 3, 3, outputs, frames * across), f32),
             totals,
             pltpu.VMEM((frames, height, across, outputs), f32),
-            passed, passed, passed, passed,
+            turned, turned, passed, passed,
             pltpu.SemaphoreType.DMA((11,)),
             pltpu.SemaphoreType.DMA((4, 2)),
             pltpu.SemaphoreType.DMA((4, 2)),

time: 19.5 us -> 19.8 us (1.015)
  Pallas kernels: 17.7 us -> 17.9 us
    pallas_call x1, Pallas kernels: 17.7 us -> 17.9 us  [per_device(): pl.pallas_call(functools.partial(kernel, counts), out_shape=jax.ShapeDtyp...]
where the time goes in v3:
time: 19.8 us; the launch traced here: 19.6 us
  Pallas kernels  17.9 us (90%)
  local copies, waits for them, and re-layouts  1.67 us (8%)
    pallas_call x1, Pallas kernels, per_device(): pl.pallas_call(functools.partial(kernel, counts), out_shape=jax.ShapeDtyp...  17.9 us
    unnamed x1, local copies, waits for them, and re-layouts  1.67 us

profile of v3, /device:TPU:12, one launch (start us, length us, event | category | flops | bytes accessed | tf_op | source)
XLA Modules:
  0.0 19.6 jit_solution(590727107204647380)
XLA Ops:
  0.0 17.9 %block.1 = bf16[4,2,64,192]{3,2,1,0:T(8,128)(2,1)} custom-call(bf16[4,2,64,384]{3,2,1,0:T(8,128)(2,1)} %x_hbm.1, bf16[3,3,3,192,384]{4,3,2,1,0:T(8,128)(2,1)} %bitcast.2, f32[192]{0:T(256)} %b1_hbm.1, f32[384]{0:T(512)} %g1_hbm.1, bf16[3,3,3,192,192]{4,3,2,1,0:T(8,128)(2,1)} %w2_hbm.1, f32[192]{0:T(256)} %b2_hbm.1, f32[192]{0:T(256)} %g2_hbm.1, ...), custom_call_target="tpu_custom_call" | custom-call | tf_op jit(solution)/shard_map/block/pallas_call | solution.py:305
  18.0 1.7 %copy.11 = bf16[4,2,64,192]{3,2,1,0:T(8,128)(2,1)} copy(bf16[4,2,64,192]{3,2,1,0:T(8,128)(2,1)} %block.1) | data formatting | bytes 393216

commit v4 on v3

--- a/solution.py
+++ b/solution.py
@@ -180,11 +180,12 @@
             value = times_rows(weight.reshape(-1, 2 * inputs), cells)
             s1[r, i] = value.reshape(3, outputs, -1)
 
-    def halo1(i):
-        for r in range(2):
-            cells = h1[r].reshape(-1, inputs)
+    def halo1(i, span):
+        cut = slice(span[0] * across, span[1] * across)
+        for r in range(2):
+            cells = h1[r, span[0] : span[1]].reshape(-1, inputs)
             value = times_rows(w1[i, 2 * r].reshape(-1, inputs), cells)
-            s1[r, i] += value.reshape(3, outputs, -1)
+            s1[r, i, :, :, cut] += value.reshape(3, outputs, -1)
 
     def turned(r, k, half):
         return pltpu.roll(s1[r, 1, k, :, half * pair : (half + 1) * pair], across, 1)
@@ -251,13 +252,15 @@
         loads[1 + i].wait()
         local1(i)
     receive_rows(0, late_span)
-    receive_rows(0, early_span)
-    halo1(0)
-    halo1(1)
+    halo1(0, late_span)
+    halo1(1, late_span)
     send_time(0)
     loads[3].wait()
     local1(2)
-    halo1(2)
+    receive_rows(0, early_span)
+    halo1(0, early_span)
+    halo1(1, early_span)
+    halo1(2, whole)
     second_act(1)
     send_rows(1, late_span)
 
@@ -267,13 +270,13 @@
     loads[4].wait()
     skip[...] = times_rows(x[...].reshape(-1, inputs), ws[...]).reshape(skip.shape)
 
-    pl.when(has_before)(time_copy(0).wait_recv)
-    second_act(0)
-    send_rows(1, early_span)
     receive_rows(1, late_span)
     halo2(0, late_span)
     halo2(1, late_span)
     send_time(1)
+    pl.when(has_before)(time_copy(0).wait_recv)
+    second_act(0)
+    send_rows(1, early_span)
     local2(2, whole)
     for i in range(2):
         local2(i, early_span)
@@ -304,7 +307,7 @@
     turned = pltpu.VMEM((height, outputs, 2 * across), bf16)
     return pl.pallas_call(
         functools.partial(kernel, counts),
-        out_shape=jax.ShapeDtypeStruct((frames, height, across, outputs), bf16),
+        out_shape=pltpu.VMEM((frames, height, across, outputs), bf16),
         in_specs=[hbm] * 9,
         out_specs=vmem,
         scratch_shapes=[
@@ -332,7 +335,7 @@
             pltpu.SemaphoreType.DMA((2,)),
         ],
         compiler_params=pltpu.CompilerParams(
-            collective_id=0, has_side_effects=True, vmem_limit_bytes=64 * 1024 * 1024
+            collective_id=0, has_side_effects=True, vmem_limit_bytes=63 * 1024 * 1024
         ),
         name="block",
     )(

time: 19.8 us -> 17.7 us (0.89)
  the two profiles are of different devices: /device:TPU:12 before, /device:TPU:1 now
where the time goes in v4:
time: 17.7 us; the launch traced here: 17.5 us
  Pallas kernels  16.8 us (95%)
  local copies, waits for them, and re-layouts  0.71 us (4%)
    pallas_call x1, Pallas kernels, per_device(): pl.pallas_call(functools.partial(kernel, counts), out_shape=pltpu.VMEM((f...  16.8 us
    unnamed x1, local copies, waits for them, and re-layouts  0.71 us

profile of v4, /device:TPU:1, one launch (start us, length us, event | category | flops | bytes accessed | tf_op | source)
XLA Modules:
  0.0 17.5 jit_solution(8921031391826102917)
XLA Ops:
  0.0 16.8 %block.1 = bf16[4,2,64,192]{3,2,1,0:T(8,128)(2,1)S(1)} custom-call(bf16[4,2,64,384]{3,2,1,0:T(8,128)(2,1)} %x_hbm.1, bf16[3,3,3,192,384]{4,3,2,1,0:T(8,128)(2,1)} %bitcast.2, f32[192]{0:T(256)} %b1_hbm.1, f32[384]{0:T(512)} %g1_hbm.1, bf16[3,3,3,192,192]{4,3,2,1,0:T(8,128)(2,1)} %w2_hbm.1, f32[192]{0:T(256)} %b2_hbm.1, f32[192]{0:T(256)} %g2_hbm.1, ...), custom_call_target="tpu_custom_call" | custom-call | tf_op jit(solution)/shard_map/block/pallas_call | solution.py:308
  16.8 0.7 %copy.11 = bf16[4,2,64,192]{3,2,1,0:T(8,128)(2,1)} copy(bf16[4,2,64,192]{3,2,1,0:T(8,128)(2,1)S(1)} %block.1) | data formatting | bytes 393216
